TPU v7x, 128 devices: a whole 4x4x4 slice. The times are simulated.
128 devices in a mesh: group: 8 (over x, core), tp: 16 (over y, z).
Axes of the slice: x: 4, y: 4, z: 4, core: 2. Of those that a mesh axis runs over, the one named last changes fastest.
Arguments:
- prefill_in: bfloat16 [4096, 8192], P('group', 'tp'), may hold values from -6 to 6
- decode_in: bfloat16 [2, 128, 8192], P(None, 'group', 'tp'), may hold values from -6 to 6
- norm_gain: bfloat16 [8192], replicated, may hold values from 0.25 to 1.75
- query_weight: bfloat16 [8192, 8192], P(None, 'tp'), may hold values from -0.0625 to 0.0625
- query_bias: bfloat16 [8192], P('tp'), may hold values from -8 to 8
- keyval_weight: bfloat16 [8192, 2, 1024], P(None, None, 'tp'), may hold values from -0.0625 to 0.0625
- keyval_bias: bfloat16 [2, 1024], P(None, 'tp'), may hold values from -8 to 8
- out_weight: bfloat16 [8192, 8192], P('tp'), may hold values from -0.0625 to 0.0625
- pass_offset: int32 [8], P('group'), may hold values from 0 to 4095
- routing: int32 [256, 1], P('group'), may hold values from 0 to 7; in each aligned block of 32 rows (0 to 31, 32 to 63, ...) at most 8 rows name the same one
- cache_len: int32 [128], P('group'), may hold values from 1 to 256, as said below
- page_table: int32 [128, 8], P('group'), may hold values from 0 to 63
- cache_keyval: bfloat16 [128, 256, 2, 1024], P('group', None, None, 'tp'), may hold values from -6 to 6
Outputs:
- prefill_out: bfloat16 [4096, 8192], P('group', 'tp')
- decode_out: bfloat16 [2, 128, 8192], P(None, 'group', 'tp')
Inputs may be any that keep to these rules, and one draw needn't show every extreme that they name: `routing`: among the blocks of one group (aligned blocks of 32 rows) no group is named more than 8 times, a bound that some block reaches. `cache_len`: the first row of each group of 16 rows has length 256.
All inputs are finite; a program needn't handle non-finite values.
Results may differ from a plain program's by a relative error of at most 0.015.
Values may be sent and summed in bfloat16 or wider, within the bound.
A program may use at most 128 MiB of HBM per device.

v0:
```python
import jax
import jax.numpy as jnp
import numpy as np
from jax import lax
from jax.experimental import pallas as pl
from jax.experimental.pallas import tpu as pltpu
from jax.sharding import PartitionSpec as P

MESH = pl.DeviceIdType.MESH
F32 = jnp.float32
BF16 = jnp.bfloat16
HD = 128
FS = 512
C0, C1 = 288, 256
DEC = 32
NEG_FILL = -1e30
EPSILON = 1e-06
CACHE = 256
WIDTH = 8192


def nt(a, b):
    return lax.dot_general(a, b, (((1,), (1,)), ((), ())), preferred_element_type=F32)


def mm(a, b):
    return jnp.dot(a, b, preferred_element_type=F32)


def offset_of(k):
    return k + k // 2 - 2 * (k // 3)


def kernel(
    pre_in, dec_in, gain, qbias, kvbias, freq, offset, routing, lens, table,
    wq_hbm, wkv_hbm, wo_hbm, cache_hbm,
    pre_out, dec_out,
    params, x0, x1, wq, wkv, wo, acc0, acc1, ss0, ss1, cos_t, sin_t,
    q0, q1, kvs0, kvs1, kvr0, kvr1, kv, kvd, att0, att1, attd,
    cache, s8, sx, e_own, ex, o8, ox, m_c, l_c, pack, pool, cnt_s, cnt_r, qx, mult,
    tok_slot,
    rs0, rs1, rsd,
    w_sem, ag_send, ag_recv, rs_send, rs_recv, pair_send, pair_recv, grp_send, grp_recv,
):
    g = lax.axis_index("group")
    t = lax.axis_index("tp")
    core = g % 2
    y, z = t // 4, t % 4
    f = z + core * (y - z)
    s = y + core * (z - y)

    def tp_of(ff, ss):
        return 4 * ss + ff + core * 3 * (ff - ss)

    fn, fp = tp_of((f + 1) % 4, s), tp_of((f + 3) % 4, s)
    sn, sp = tp_of(f, (s + 1) % 4), tp_of(f, (s + 3) % 4)
    pair = t + 1 - 2 * (t % 2)
    half = t % 2

    drows = dec_in[...].astype(F32)
    drows = jnp.concatenate([drows[0:8], drows[16:24], drows[8:16], drows[24:32]], axis=0)
    first = jnp.concatenate([drows.astype(BF16), pre_in[0:256]], axis=0)
    x0[0] = first.reshape(2, C0 // 2, FS)
    x1[0] = pre_in[256:512].reshape(2, C1 // 2, FS)

    barrier = pltpu.get_barrier_semaphore()
    for peer in (fn, fp, sn, sp):
        pl.semaphore_signal(barrier, inc=1, device_id=(g, peer), device_id_type=MESH)
    for j in range(1, 8):
        pl.semaphore_signal(barrier, inc=1, device_id=((g + j) % 8, t), device_id_type=MESH)

    loads = [
        pltpu.make_async_copy(wq_hbm, wq, w_sem.at[0]),
        pltpu.make_async_copy(wkv_hbm, wkv, w_sem.at[1]),
        pltpu.make_async_copy(wo_hbm, wo, w_sem.at[2]),
        pltpu.make_async_copy(cache_hbm, cache, w_sem.at[3]),
    ]
    for load in loads:
        load.start()

    pl.semaphore_wait(barrier, 11)

    def to_tp(src, dst, send, recv, peer):
        return pltpu.make_async_remote_copy(src, dst, send, recv, device_id=(g, peer), device_id_type=MESH)

    class Gather:
        def __init__(self, x, rows, c):
            self.x, self.c, self.sent = x, c, []

        def copy(self, src, dst, part, index, peer):
            src, dst = 4 * src[0] + src[1], 4 * dst[0] + dst[1]
            src = self.x.at[src] if part is None else self.x.at[src, part]
            dst = self.x.at[dst] if part is None else self.x.at[dst, part]
            return to_tp(src, dst, ag_send.at[self.c, index], ag_recv.at[self.c, index], peer)

        def go(self, src, dst, part, index, peer):
            copy = self.copy(src, dst, part, index, peer)
            copy.start()
            self.sent.append(copy)

        def came(self, dst, part, index):
            self.copy(dst, dst, part, index, fn).wait_recv()

        def send_own(self):
            self.go((0, 0), (2, 0), None, 0, fn)
            self.go((0, 0), (1, 0), None, 1, fp)
            self.line(0)

        def line(self, k):
            self.go((k, 0), (k, 2), None, 4 + 4 * k, sn)
            self.go((k, 0), (k, 1), None, 5 + 4 * k, sp)

        def near(self):
            self.came((2, 0), None, 0)
            self.go((2, 0), (3, 0), 0, 2, fn)
            self.line(2)
            self.came((1, 0), None, 1)
            self.go((1, 0), (3, 0), 1, 3, fp)
            self.line(1)

        def far(self):
            self.came((3, 0), 0, 2)
            self.came((3, 0), 1, 3)
            self.line(3)

        def step(self, i):
            j, w = (i - 3) // 3, (i - 3) % 3
            if i < 3:
                if i == 1:
                    self.near()
                return i, 0
            if i == 5:
                self.far()
                return 3, 0
            if i == 15 or w == 2:
                self.came((j - 1, 3), 0, 2 + 4 * j)
                self.came((j - 1, 3), 1, 3 + 4 * j)
                return j - 1, 3
            if w == 0:
                self.came((j, 2), None, 4 + 4 * j)
                self.go((j, 2), (j, 3), 0, 6 + 4 * j, sn)
                return j, 2
            self.came((j, 1), None, 5 + 4 * j)
            self.go((j, 1), (j, 3), 1, 7 + 4 * j, sp)
            return j, 1

        def drain(self):
            for copy in self.sent:
                copy.wait_send()

    ag0, ag1 = Gather(x0, C0, 0), Gather(x1, C1, 1)
    ag0.send_own()
    ag1.send_own()

    def accumulate(x, acc, ss, place):
        kf, ks = place
        slot = tp_of((f + offset_of(kf)) % 4, (s + offset_of(ks)) % 4)
        at = pl.multiple_of(slot * FS, FS)
        xf = x[4 * kf + ks].reshape(-1, FS).astype(F32)
        sq = xf * xf
        ss[...] += sq[:, 0:128] + sq[:, 128:256] + sq[:, 256:384] + sq[:, 384:512]
        xg = (xf * params[pl.ds(slot, 1), :]).astype(BF16)
        acc[:, 0:512] += mm(xg, wq[pl.ds(at, FS), :])
        acc[:, 512:640] += nt(xg, wkv[:, pl.ds(at, FS)])

    for i in range(16):
        params[i:i + 1] = gain[i * FS:(i + 1) * FS].astype(F32).reshape(1, FS)
    params[16:17] = qbias[...].astype(F32).reshape(1, FS)
    params[17:18, 0:HD] = jnp.concatenate([kvbias[0:1].astype(F32), kvbias[1:2].astype(F32)], axis=1)
    acc0[...] = jnp.zeros_like(acc0)
    acc1[...] = jnp.zeros_like(acc1)
    ss0[...] = jnp.zeros_like(ss0)
    ss1[...] = jnp.zeros_like(ss1)
    loads[0].wait()
    loads[1].wait()

    gathers = ((ag0, x0, acc0, ss0), (ag1, x1, acc1, ss1))

    def advance(c, *steps):
        ag, x, acc, ss = gathers[c]
        for place in [ag.step(i) for i in steps]:
            accumulate(x, acc, ss, place)

    advance(0, 0, 1, 2, 3, 4)
    advance(0, 5)

    advance(1, 0, 1, 2, 3, 4)
    advance(0, 6, 7, 8)
    advance(1, 5)
    advance(0, 9, 10, 11)
    advance(1, 6, 7, 8)
    advance(0, 12, 13)

    lane = lax.broadcasted_iota(jnp.int32, (C0, HD), 1)
    row = lax.broadcasted_iota(jnp.int32, (C0, HD), 0)
    places = row - DEC + offset[0]
    for r in range(16):
        base = (r // 8) * 16 + r % 8
        places = jnp.where(row == base, lens[r], places)
        places = jnp.where(row == base + 8, lens[r] + 1, places)
    sign = jnp.where(lane < 64, -1.0, 1.0).astype(F32)
    angle = places.astype(F32) * freq[...]
    cos_t[0:C0] = jnp.cos(angle)
    sin_t[0:C0] = jnp.sin(angle) * sign
    angle = (row[0:C1] + (C1 + offset[0])).astype(F32) * freq[...]
    cos_t[C0:C0 + C1] = jnp.cos(angle)
    sin_t[C0:C0 + C1] = jnp.sin(angle) * sign[0:C1]

    token = lax.broadcasted_iota(jnp.int32, (8, 512), 1)

    def rank_block(b, carry):
        slots, counts = carry
        d = routing[b]
        rank = jnp.int32(0)
        for k in range(8):
            rank = rank + jnp.where(d == k, counts[k], 0)
        slots = jnp.where(token // 16 == b, d * 128 + rank * 16 + token % 16, slots)
        return slots, tuple(counts[k] + jnp.where(d == k, 1, 0) for k in range(8))

    slots, counts = lax.fori_loop(
        0, 32, rank_block, (jnp.zeros((8, 512), jnp.int32), (jnp.int32(0),) * 8)
    )
    tok_slot[...] = slots
    for k in range(8):
        cnt_s[k] = jnp.full((8, 128), 1.0, F32) * counts[k].astype(F32)

    page = lax.broadcasted_iota(jnp.int32, (16, 1024), 1) // 16
    prow = lax.broadcasted_iota(jnp.int32, (16, 1024), 0)

    def count_pages(i, times):
        r, j = i // 8, i % 8
        return times + jnp.where((prow == r) & (page == table[j, r]), 1.0, 0.0)

    mult[...] = lax.fori_loop(0, 128, count_pages, jnp.zeros((16, 1024), F32))

    advance(0, 14, 15)

    def finish(acc, ss, kvs, q, table_at, rows):
        inv = lax.rsqrt(jnp.sum(ss[...], axis=1, keepdims=True) * (1.0 / WIDTH) + EPSILON)
        kvs[...] = (acc[:, 512:640] * inv + params[17:18, 0:HD]).astype(BF16)
        return inv

    def finish_q(acc, ss, q, table_at, rows):
        inv = lax.rsqrt(jnp.sum(ss[...], axis=1, keepdims=True) * (1.0 / WIDTH) + EPSILON)
        c, sn_ = cos_t[table_at:table_at + rows], sin_t[table_at:table_at + rows]
        for h in range(4):
            at = slice(h * HD, (h + 1) * HD)
            v = acc[:, at] * inv + params[16:17, at]
            q[:, at] = (v * c + pltpu.roll(v, 64, 1) * sn_).astype(BF16)

    def join(own, other, table_at, rows):
        a, b = own[...].astype(F32), other[...].astype(F32)
        lo = jnp.where(half == 0, a, b)
        hi = jnp.where(half == 0, b, a)
        low = lax.broadcasted_iota(jnp.int32, (rows, HD), 1) < 64
        k = jnp.where(low, lo, pltpu.roll(hi, 64, 1))
        v = jnp.where(low, pltpu.roll(lo, 64, 1), hi)
        k = k * cos_t[table_at:table_at + rows] + pltpu.roll(k, 64, 1) * sin_t[table_at:table_at + rows]
        return k.astype(BF16), v.astype(BF16)

    def pair_copy(src, dst, index):
        return to_tp(src, dst, pair_send.at[index], pair_recv.at[index], pair)

    kv_join = [pair_copy(kvs0, kvr0, 0), pair_copy(kvs1, kvr1, 1)]
    q_swap = pair_copy(q0.at[pl.ds(0, DEC)], qx, 2)
    s_swap = pair_copy(s8.at[pl.ds(HD, HD)], sx, 3)
    e_swap = pair_copy(e_own, ex, 4)
    o_swap = pair_copy(o8.at[pl.ds(HD, HD)], ox, 5)

    scale = HD ** (-0.5)

    def attend(q, start, att, h, keys):
        at = pl.ds(h * HD, HD)
        sc = nt(q[start:start + 256, at], kv[0:keys, 0:HD]) * scale
        qi = lax.broadcasted_iota(jnp.int32, (256, keys), 0) + (keys - 256)
        ki = lax.broadcasted_iota(jnp.int32, (256, keys), 1)
        sc = jnp.where(ki <= qi, sc, NEG_FILL)
        e = jnp.exp(sc - jnp.max(sc, axis=1, keepdims=True))
        total = jnp.sum(e, axis=1, keepdims=True)
        att[:, at] = (mm(e.astype(BF16), kv[0:keys, HD:2 * HD]) / total).astype(BF16)

    def query_row(shape):
        m = lax.broadcasted_iota(jnp.int32, shape, 0)
        return m % DEC // 16 * 8 + m % 8

    def by_head(ref):
        return jnp.concatenate([ref[0:DEC, h * HD:(h + 1) * HD] for h in range(4)], axis=0)

    def padded(part):
        zero = jnp.zeros((64, CACHE), BF16)
        return jnp.where(half == 0, jnp.concatenate([part, zero], axis=0), jnp.concatenate([zero, part], axis=0))

    def cache_scores():
        q_swap.wait_recv()
        loads[3].wait()
        q8 = jnp.concatenate([by_head(q0), by_head(qx)], axis=0)
        s8[...] = jnp.zeros_like(s8)

        @pl.loop(0, 16)
        def _(r):
            s8[...] = jnp.where(query_row((256, CACHE)) == r, mm(q8, padded(cache[r, 0])), s8[...])

        s_swap.start()

    def cache_weights():
        s_swap.wait_recv()
        owner = query_row((HD, CACHE))
        length = jnp.zeros((HD, CACHE), jnp.int32)
        for r in range(16):
            length = jnp.where(owner == r, lens[r], length)
        sc = (s8[0:HD] + sx[...]) * scale
        sc = jnp.where(lax.broadcasted_iota(jnp.int32, (HD, CACHE), 1) < length, sc, NEG_FILL)
        top = jnp.max(sc, axis=1, keepdims=True)
        e = jnp.exp(sc - top)
        m_c[...] = jnp.broadcast_to(top, (HD, HD))
        l_c[...] = jnp.broadcast_to(jnp.sum(e, axis=1, keepdims=True), (HD, HD))
        e_own[...] = e.astype(BF16)
        e_swap.start()

    def cache_values():
        e_swap.wait_recv()
        e8 = jnp.concatenate([e_own[...], ex[...]], axis=0)
        o8[...] = jnp.zeros_like(o8)

        @pl.loop(0, 16)
        def _(r):
            o8[...] = jnp.where(query_row((256, HD)) == r, nt(e8, padded(cache[r, 1])), o8[...])

        o_swap.start()

    def pass_keys(c, kvs, kvr, at, rows):
        kv_join[c].wait_recv()
        k, v = join(kvs, kvr, at, rows)
        if c == 0:
            kvd[:, 0:HD] = k[0:DEC]
            kvd[:, HD:2 * HD] = v[0:DEC]
            k, v = k[DEC:C0], v[DEC:C0]
        kv[256 * c:256 * (c + 1), 0:HD] = k
        kv[256 * c:256 * (c + 1), HD:2 * HD] = v

    class Scatter:
        def __init__(self, bufs, att, rows, c):
            (self.s1, self.ra, self.rb, self.s2p, self.s2m, self.rm, self.rp,
             self.s3, self.fa, self.fb, self.gm, self.gp) = bufs
            self.att, self.c = att, c
            if rows == DEC:
                self.up = (slice(None), pl.ds(0, FS // 2))
                self.lo = (slice(None), pl.ds(FS // 2, FS // 2))
            else:
                self.up = (pl.ds(0, rows // 2), slice(None))
                self.lo = (pl.ds(rows // 2, rows // 2), slice(None))

        def term(self, kf, ks):
            slot = tp_of((f + offset_of(kf)) % 4, (s + offset_of(ks)) % 4)
            return mm(self.att[...], wo[:, pl.ds(pl.multiple_of(slot * FS, FS), FS)])

        def copy(self, src, dst, index, peer):
            return to_tp(src, dst, rs_send.at[self.c, index], rs_recv.at[self.c, index], peer)

        def merge(self, p, part, upper):
            axis = 1 if p.shape[0] == DEC else 0
            n = p.shape[axis] // 2
            a, b = lax.slice_in_dim(p, 0, n, axis=axis), lax.slice_in_dim(p, n, 2 * n, axis=axis)
            if upper:
                a = a + part.astype(F32)
            else:
                b = b + part.astype(F32)
            return jnp.concatenate([a, b], axis=axis).astype(BF16)

        def upper(self, k):
            return self.copy(self.s1.at[(k, *self.up)], self.ra.at[k], 4 * k, sn)

        def lower(self, k):
            return self.copy(self.s1.at[(k, *self.lo)], self.rb.at[k], 4 * k + 1, sp)

        def ahead(self, k):
            return self.copy(self.s2p.at[k], self.rm.at[k], 4 * k + 2, sn)

        def back(self, k):
            return self.copy(self.s2m.at[k], self.rp.at[k], 4 * k + 3, sp)

        def last(self):
            return [
                self.copy(self.s3.at[(0, *self.up)], self.fa, 16, fn),
                self.copy(self.s3.at[(0, *self.lo)], self.fb, 17, fp),
                self.copy(self.s3.at[1], self.gm, 18, fn),
                self.copy(self.s3.at[2], self.gp, 19, fp),
            ]

        def first_hop(self):
            @pl.loop(0, 4)
            def _(j):
                k = 3 - j
                self.s1[k] = self.term(k, 3).astype(BF16)
                self.upper(k).start()
                self.lower(k).start()

        def second_hop(self):
            @pl.loop(0, 4)
            def _(j):
                k = 3 - j
                p = self.term(k, 1)
                self.upper(k).wait_recv()
                self.s2p[k] = self.merge(p, self.ra[k], True)
                self.ahead(k).start()
                p = self.term(k, 2)
                self.lower(k).wait_recv()
                self.s2m[k] = self.merge(p, self.rb[k], False)
                self.back(k).start()

        def gathered(self, k):
            p = self.term(k, 0)
            self.ahead(k).wait_recv()
            self.back(k).wait_recv()
            return p + self.rm[k].astype(F32) + self.rp[k].astype(F32)

        def third_hop(self):
            c1, c2, c3, c4 = self.last()
            self.s3[0] = self.gathered(3).astype(BF16)
            c1.start()
            c2.start()
            p = self.gathered(1)
            c1.wait_recv()
            self.s3[1] = self.merge(p, self.fa[...], True)
            c3.start()
            p = self.gathered(2)
            c2.wait_recv()
            self.s3[2] = self.merge(p, self.fb[...], False)
            c4.start()

        def result(self):
            _, _, c3, c4 = self.last()
            p = self.gathered(0)
            c3.wait_recv()
            c4.wait_recv()
            return p + self.gm[...].astype(F32) + self.gp[...].astype(F32)

        def drain(self):
            for k in range(4):
                for c in (self.upper(k), self.lower(k), self.ahead(k), self.back(k)):
                    c.wait_send()
            for c in self.last():
                c.wait_send()

    sc0, sc1, scd = Scatter(rs0, att0, 256, 0), Scatter(rs1, att1, 256, 1), Scatter(rsd, attd, DEC, 2)

    def group_copies(j):
        there = (g + j) % 8
        dev = (there, t)
        return (
            pltpu.make_async_remote_copy(pack.at[j], pool.at[j], grp_send.at[0, j], grp_recv.at[0, j],
                                         device_id=dev, device_id_type=MESH),
            pltpu.make_async_remote_copy(cnt_s.at[there], cnt_r.at[j], grp_send.at[1, j], grp_recv.at[1, j],
                                         device_id=dev, device_id_type=MESH),
        )

    def send_pages():
        @pl.loop(0, 8)
        def _(j):
            there = (g + j) % 8
            want = lax.broadcasted_iota(jnp.int32, (128, 512), 0) + there * 128
            hot = jnp.where(tok_slot[0:1, :] == want, 1.0, 0.0).astype(BF16)
            pages = mm(hot, kv[...]).astype(BF16)

            @pl.when(j == 0)
            def _():
                pool[0] = pages
                cnt_r[0] = cnt_s[there]

            @pl.when(j > 0)
            def _():
                pack[j] = pages
                for c in group_copies(j):
                    c.start()

    def decode_rows():
        @pl.loop(1, 8)
        def _(j):
            for c in group_copies(j):
                c.wait_recv()

        qa = by_head(q0)
        scores, weight = [], []
        for src in range(8):
            sc = nt(qa, pool[src, :, 0:HD]) * scale
            slot = lax.broadcasted_iota(jnp.int32, (16, HD), 1) // 16
            at = pl.multiple_of((g + 8 - src) % 8 * HD, HD)
            m16 = jnp.where(slot.astype(F32) < cnt_r[src, 0:1], mult[:, pl.ds(at, HD)], 0.0)
            m = jnp.concatenate([m16[0:8], m16[0:8], m16[8:16], m16[8:16]] * 4, axis=0)
            weight.append(m)
            scores.append(jnp.where(m > 0.0, sc, NEG_FILL))
        new = jnp.concatenate([kvd[...], jnp.zeros((HD - DEC, 2 * HD), BF16)], axis=0)
        col = lax.broadcasted_iota(jnp.int32, (HD, HD), 1)
        same = (col // 16 * 8 + col % 8 == query_row((HD, HD))) & (col < DEC)
        step = lax.broadcasted_iota(jnp.int32, (HD, HD), 0) // 8 % 2
        ok = same & (col // 8 % 2 <= step)
        scores.append(jnp.where(ok, nt(qa, new[:, 0:HD]) * scale, NEG_FILL))
        top = m_c[...]
        for sc in scores:
            top = jnp.maximum(top, jnp.max(sc, axis=1, keepdims=True))
        o_swap.wait_recv()
        old = jnp.exp(m_c[...] - top)
        total = l_c[...] * old
        mixed = (o8[0:HD] + ox[...]) * old
        for i in range(9):
            e = jnp.exp(scores[i] - top)
            if i < 8:
                e = e * weight[i]
            total = total + jnp.sum(e, axis=1, keepdims=True)
            values = pool[i, :, HD:2 * HD] if i < 8 else new[:, HD:2 * HD]
            mixed = mixed + mm(e.astype(BF16), values)
        mixed = (mixed / total).astype(BF16)
        for h in range(4):
            attd[:, h * HD:(h + 1) * HD] = mixed[h * DEC:(h + 1) * DEC]

    finish(acc0, ss0, kvs0, q0, 0, C0)
    kv_join[0].start()
    finish_q(acc0, ss0, q0, 0, C0)
    q_swap.start()
    advance(1, 9, 10, 11)
    pass_keys(0, kvs0, kvr0, 0, C0)
    for h in range(4):
        attend(q0, DEC, att0, h, 256)
    loads[2].wait()
    sc0.first_hop()
    advance(1, 12, 13)
    cache_scores()
    advance(1, 14, 15)
    finish(acc1, ss1, kvs1, q1, C0, C1)
    kv_join[1].start()
    cache_weights()
    finish_q(acc1, ss1, q1, C0, C1)
    sc0.second_hop()
    pass_keys(1, kvs1, kvr1, C0, C1)
    send_pages()
    cache_values()
    for h in range(4):
        attend(q1, 0, att1, h, 512)
    sc1.first_hop()
    sc0.third_hop()
    decode_rows()
    scd.first_hop()
    sc1.second_hop()
    scd.second_hop()
    pre_out[0:256] = (sc0.result() + pre_in[0:256].astype(F32)).astype(BF16)
    sc1.third_hop()
    scd.third_hop()
    pre_out[256:512] = (sc1.result() + pre_in[256:512].astype(F32)).astype(BF16)
    dsum = scd.result()
    dsum = jnp.concatenate([dsum[0:8], dsum[16:24], dsum[8:16], dsum[24:32]], axis=0)
    dec_out[...] = (dsum + dec_in[...].astype(F32)).astype(BF16)

    ag0.drain()
    ag1.drain()
    sc0.drain()
    sc1.drain()
    scd.drain()
    for c in kv_join + [q_swap, s_swap, e_swap, o_swap]:
        c.wait_send()

    @pl.loop(1, 8)
    def _(j):
        for c in group_copies(j):
            c.wait_send()


def scatter_bufs(rows):
    h, w = (rows, FS // 2) if rows == DEC else (rows // 2, FS)
    return (
        pltpu.VMEM((4, rows, FS), BF16),
        pltpu.VMEM((4, h, w), BF16),
        pltpu.VMEM((4, h, w), BF16),
        pltpu.VMEM((4, rows, FS), BF16),
        pltpu.VMEM((4, rows, FS), BF16),
        pltpu.VMEM((4, rows, FS), BF16),
        pltpu.VMEM((4, rows, FS), BF16),
        pltpu.VMEM((3, rows, FS), BF16),
        pltpu.VMEM((h, w), BF16),
        pltpu.VMEM((h, w), BF16),
        pltpu.VMEM((rows, FS), BF16),
        pltpu.VMEM((rows, FS), BF16),
    )


def body(
    prefill_in, decode_in, norm_gain, query_weight, query_bias, keyval_weight, keyval_bias,
    out_weight, pass_offset, routing, cache_len, page_table, cache_keyval,
):
    half_lanes = np.arange(HD) % 64
    freq = jnp.asarray((1000000.0 ** (-(half_lanes * (2.0 / HD)))).astype(np.float32).reshape(1, HD))
    vmem = pl.BlockSpec(memory_space=pltpu.VMEM)
    smem = pl.BlockSpec(memory_space=pltpu.SMEM)
    hbm = pl.BlockSpec(memory_space=pl.ANY)
    pre, dec = pl.pallas_call(
        kernel,
        out_shape=(
            jax.ShapeDtypeStruct((512, FS), BF16),
            jax.ShapeDtypeStruct((DEC, FS), BF16),
        ),
        in_specs=[vmem] * 6 + [smem] * 4 + [hbm] * 4,
        out_specs=(vmem, vmem),
        scratch_shapes=[
            pltpu.VMEM((18, FS), F32),
            pltpu.VMEM((16, 2, C0 // 2, FS), BF16),
            pltpu.VMEM((16, 2, C1 // 2, FS), BF16),
            pltpu.VMEM((WIDTH, FS), BF16),
            pltpu.VMEM((HD, WIDTH), BF16),
            pltpu.VMEM((FS, WIDTH), BF16),
            pltpu.VMEM((C0, 640), F32),
            pltpu.VMEM((C1, 640), F32),
            pltpu.VMEM((C0, HD), F32),
            pltpu.VMEM((C1, HD), F32),
            pltpu.VMEM((C0 + C1, HD), F32),
            pltpu.VMEM((C0 + C1, HD), F32),
            pltpu.VMEM((C0, FS), BF16),
            pltpu.VMEM((C1, FS), BF16),
            pltpu.VMEM((C0, HD), BF16),
            pltpu.VMEM((C1, HD), BF16),
            pltpu.VMEM((C0, HD), BF16),
            pltpu.VMEM((C1, HD), BF16),
            pltpu.VMEM((512, 2 * HD), BF16),
            pltpu.VMEM((DEC, 2 * HD), BF16),
            pltpu.VMEM((256, FS), BF16),
            pltpu.VMEM((256, FS), BF16),
            pltpu.VMEM((DEC, FS), BF16),
            pltpu.VMEM((16, 2, 64, CACHE), BF16),
            pltpu.VMEM((256, CACHE), F32),
            pltpu.VMEM((HD, CACHE), F32),
            pltpu.VMEM((HD, CACHE), BF16),
            pltpu.VMEM((HD, CACHE), BF16),
            pltpu.VMEM((256, HD), F32),
            pltpu.VMEM((HD, HD), F32),
            pltpu.VMEM((HD, HD), F32),
            pltpu.VMEM((HD, HD), F32),
            pltpu.VMEM((8, HD, 2 * HD), BF16),
            pltpu.VMEM((8, HD, 2 * HD), BF16),
            pltpu.VMEM((8, 8, HD), F32),
            pltpu.VMEM((8, 8, HD), F32),
            pltpu.VMEM((DEC, FS), BF16),
            pltpu.VMEM((16, 1024), F32),
            pltpu.VMEM((8, 512), jnp.int32),
            scatter_bufs(256),
            scatter_bufs(256),
            scatter_bufs(DEC),
            pltpu.SemaphoreType.DMA((4,)),
            pltpu.SemaphoreType.DMA((2, 20)),
            pltpu.SemaphoreType.DMA((2, 20)),
            pltpu.SemaphoreType.DMA((3, 20)),
            pltpu.SemaphoreType.DMA((3, 20)),
            pltpu.SemaphoreType.DMA((6,)),
            pltpu.SemaphoreType.DMA((6,)),
            pltpu.SemaphoreType.DMA((2, 8)),
            pltpu.SemaphoreType.DMA((2, 8)),
        ],
        compiler_params=pltpu.CompilerParams(
            collective_id=0, has_side_effects=True, vmem_limit_bytes=62 * 2**20
        ),
    )(
        prefill_in,
        decode_in.reshape(DEC, FS),
        norm_gain,
        query_bias,
        keyval_bias,
        freq,
        pass_offset,
        routing.reshape(32),
        cache_len,
        page_table.T,
        query_weight,
        keyval_weight.transpose(1, 2, 0).reshape(HD, WIDTH),
        out_weight,
        cache_keyval.transpose(0, 2, 3, 1),
    )
    return pre, dec.reshape(2, 16, FS)


def solution(mesh):
    in_specs = (
        P("group", "tp"),
        P(None, "group", "tp"),
        P(),
        P(None, "tp"),
        P("tp"),
        P(None, None, "tp"),
        P(None, "tp"),
        P("tp", None),
        P("group"),
        P("group", None),
        P("group"),
        P("group", None),
        P("group", None, None, "tp"),
    )
    out_specs = (P("group", "tp"), P(None, "group", "tp"))
    return jax.shard_map(body, mesh=mesh, in_specs=in_specs, out_specs=out_specs, check_vma=False)
```

profile of v0, /device:TPU:1, one launch (start us, length us, event | category | flops | bytes accessed | tf_op | source)
XLA Modules:
  0.0 124.2 jit_solution(16198389757644879947)
XLA Ops:
  1.3 119.7 %shard_map.149 = (bf16[512,512]{1,0:T(8,128)(2,1)}, bf16[32,512]{1,0:T(8,128)(2,1)}) custom-call(bf16[512,512]{1,0:T(8,128)(2,1)} %pre_in.1, bf16[32,512]{1,0:T(8,128)(2,1)} %bitcast.10, bf16[8192]{0:T(1024)(128)(2,1)} %gain.1, bf16[512]{0:T(512)(128)(2,1)} %qbias.1, bf16[2,64]{1,0:T(2,128)(2,1)} %kvbias.1, f32[1,128]{1,0:T(1,128)} %constant.2.clone.freq, ...), custom_call_target="tpu_custom_call" | custom-call | tf_op jit(solution)/shard_map/pallas_call | solution.py:594
  121.0 1.9 %copy.19 = bf16[512,512]{1,0:T(8,128)(2,1)} copy(bf16[512,512]{1,0:T(8,128)(2,1)} %get-tuple-element.8) | data formatting | bytes 1048576
  122.9 1.4 %copy.20 = bf16[2,16,512]{2,1,0:T(8,128)(2,1)} copy(bf16[2,16,512]{2,1,0:T(8,128)(2,1)} %bitcast.11) | data formatting | bytes 65536
where the time goes:
time: 125 us; the launch traced here: 124 us
  Pallas kernels  120 us (96%)
  local copies, waits for them, and re-layouts  3.24 us (3%)
  between operations  1.29 us (1%)
    pallas_call x1, Pallas kernels, body(): pl.pallas_call(kernel, out_shape=(jax.ShapeDtypeStruct((512, FS), BF16),...  120 us
    unnamed x2, local copies, waits for them, and re-layouts  3.24 us

commit v1 on v0

--- a/solution.py
+++ b/solution.py
@@ -11,8 +11,9 @@
 BF16 = jnp.bfloat16
 HD = 128
 FS = 512
-C0, C1 = 288, 256
 DEC = 32
+T0, T1 = 256, 256
+C0, C1 = DEC + T0, T1
 NEG_FILL = -1e30
 EPSILON = 1e-06
 CACHE = 256
@@ -36,10 +37,10 @@
     wq_hbm, wkv_hbm, wo_hbm, cache_hbm,
     pre_out, dec_out,
     params, x0, x1, wq, wkv, wo, acc0, acc1, ss0, ss1, cos_t, sin_t,
-    q0, q1, kvs0, kvs1, kvr0, kvr1, kv, kvd, att0, att1, attd,
+    q0, q1, kvs0, kvs1, kvr0, kvr1, kv, kvd, att0, att1,
     cache, s8, sx, e_own, ex, o8, ox, m_c, l_c, pack, pool, cnt_s, cnt_r, qx, mult,
     tok_slot,
-    rs0, rs1, rsd,
+    rs0, rs1,
     w_sem, ag_send, ag_recv, rs_send, rs_recv, pair_send, pair_recv, grp_send, grp_recv,
 ):
     g = lax.axis_index("group")
@@ -59,9 +60,9 @@
 
     drows = dec_in[...].astype(F32)
     drows = jnp.concatenate([drows[0:8], drows[16:24], drows[8:16], drows[24:32]], axis=0)
-    first = jnp.concatenate([drows.astype(BF16), pre_in[0:256]], axis=0)
+    first = jnp.concatenate([drows.astype(BF16), pre_in[0:T0]], axis=0)
     x0[0] = first.reshape(2, C0 // 2, FS)
-    x1[0] = pre_in[256:512].reshape(2, C1 // 2, FS)
+    x1[0] = pre_in[T0:512].reshape(2, C1 // 2, FS)
 
     barrier = pltpu.get_barrier_semaphore()
     for peer in (fn, fp, sn, sp):
@@ -202,9 +203,10 @@
     angle = places.astype(F32) * freq[...]
     cos_t[0:C0] = jnp.cos(angle)
     sin_t[0:C0] = jnp.sin(angle) * sign
-    angle = (row[0:C1] + (C1 + offset[0])).astype(F32) * freq[...]
+    row = lax.broadcasted_iota(jnp.int32, (C1, HD), 0)
+    angle = (row + (T0 + offset[0])).astype(F32) * freq[...]
     cos_t[C0:C0 + C1] = jnp.cos(angle)
-    sin_t[C0:C0 + C1] = jnp.sin(angle) * sign[0:C1]
+    sin_t[C0:C0 + C1] = jnp.sin(angle) * sign[0:1]
 
     token = lax.broadcasted_iota(jnp.int32, (8, 512), 1)
 
@@ -269,15 +271,15 @@
 
     scale = HD ** (-0.5)
 
-    def attend(q, start, att, h, keys):
+    def attend(q, start, rows, att, h, keys):
         at = pl.ds(h * HD, HD)
-        sc = nt(q[start:start + 256, at], kv[0:keys, 0:HD]) * scale
-        qi = lax.broadcasted_iota(jnp.int32, (256, keys), 0) + (keys - 256)
-        ki = lax.broadcasted_iota(jnp.int32, (256, keys), 1)
+        sc = nt(q[start:start + rows, at], kv[0:keys, 0:HD]) * scale
+        qi = lax.broadcasted_iota(jnp.int32, (rows, keys), 0) + (keys - rows)
+        ki = lax.broadcasted_iota(jnp.int32, (rows, keys), 1)
         sc = jnp.where(ki <= qi, sc, NEG_FILL)
         e = jnp.exp(sc - jnp.max(sc, axis=1, keepdims=True))
         total = jnp.sum(e, axis=1, keepdims=True)
-        att[:, at] = (mm(e.astype(BF16), kv[0:keys, HD:2 * HD]) / total).astype(BF16)
+        att[0:rows, at] = (mm(e.astype(BF16), kv[0:keys, HD:2 * HD]) / total).astype(BF16)
 
     def query_row(shape):
         m = lax.broadcasted_iota(jnp.int32, shape, 0)
@@ -335,20 +337,17 @@
             kvd[:, 0:HD] = k[0:DEC]
             kvd[:, HD:2 * HD] = v[0:DEC]
             k, v = k[DEC:C0], v[DEC:C0]
-        kv[256 * c:256 * (c + 1), 0:HD] = k
-        kv[256 * c:256 * (c + 1), HD:2 * HD] = v
+        tokens = slice(0, T0) if c == 0 else slice(T0, 512)
+        kv[tokens, 0:HD] = k
+        kv[tokens, HD:2 * HD] = v
 
     class Scatter:
         def __init__(self, bufs, att, rows, c):
             (self.s1, self.ra, self.rb, self.s2p, self.s2m, self.rm, self.rp,
              self.s3, self.fa, self.fb, self.gm, self.gp) = bufs
             self.att, self.c = att, c
-            if rows == DEC:
-                self.up = (slice(None), pl.ds(0, FS // 2))
-                self.lo = (slice(None), pl.ds(FS // 2, FS // 2))
-            else:
-                self.up = (pl.ds(0, rows // 2), slice(None))
-                self.lo = (pl.ds(rows // 2, rows // 2), slice(None))
+            self.up = (pl.ds(0, rows // 2), slice(None))
+            self.lo = (pl.ds(rows // 2, rows // 2), slice(None))
 
         def term(self, kf, ks):
             slot = tp_of((f + offset_of(kf)) % 4, (s + offset_of(ks)) % 4)
@@ -358,7 +357,7 @@
             return to_tp(src, dst, rs_send.at[self.c, index], rs_recv.at[self.c, index], peer)
 
         def merge(self, p, part, upper):
-            axis = 1 if p.shape[0] == DEC else 0
+            axis = 0
             n = p.shape[axis] // 2
             a, b = lax.slice_in_dim(p, 0, n, axis=axis), lax.slice_in_dim(p, n, 2 * n, axis=axis)
             if upper:
@@ -442,7 +441,7 @@
             for c in self.last():
                 c.wait_send()
 
-    sc0, sc1, scd = Scatter(rs0, att0, 256, 0), Scatter(rs1, att1, 256, 1), Scatter(rsd, attd, DEC, 2)
+    sc0, sc1 = Scatter(rs0, att0, T0, 0), Scatter(rs1, att1, T1 + DEC, 1)
 
     def group_copies(j):
         there = (g + j) % 8
@@ -511,7 +510,7 @@
             mixed = mixed + mm(e.astype(BF16), values)
         mixed = (mixed / total).astype(BF16)
         for h in range(4):
-            attd[:, h * HD:(h + 1) * HD] = mixed[h * DEC:(h + 1) * DEC]
+            att1[T1:T1 + DEC, h * HD:(h + 1) * HD] = mixed[h * DEC:(h + 1) * DEC]
 
     finish(acc0, ss0, kvs0, q0, 0, C0)
     kv_join[0].start()
@@ -520,7 +519,7 @@
     advance(1, 9, 10, 11)
     pass_keys(0, kvs0, kvr0, 0, C0)
     for h in range(4):
-        attend(q0, DEC, att0, h, 256)
+        attend(q0, DEC, T0, att0, h, T0)
     loads[2].wait()
     sc0.first_hop()
     advance(1, 12, 13)
@@ -535,18 +534,16 @@
     send_pages()
     cache_values()
     for h in range(4):
-        attend(q1, 0, att1, h, 512)
-    sc1.first_hop()
+        attend(q1, 0, T1, att1, h, 512)
     sc0.third_hop()
     decode_rows()
-    scd.first_hop()
+    sc1.first_hop()
     sc1.second_hop()
-    scd.second_hop()
-    pre_out[0:256] = (sc0.result() + pre_in[0:256].astype(F32)).astype(BF16)
+    pre_out[0:T0] = (sc0.result() + pre_in[0:T0].astype(F32)).astype(BF16)
     sc1.third_hop()
-    scd.third_hop()
-    pre_out[256:512] = (sc1.result() + pre_in[256:512].astype(F32)).astype(BF16)
-    dsum = scd.result()
+    last = sc1.result()
+    pre_out[T0:512] = (last[0:T1] + pre_in[T0:512].astype(F32)).astype(BF16)
+    dsum = last[T1:T1 + DEC]
     dsum = jnp.concatenate([dsum[0:8], dsum[16:24], dsum[8:16], dsum[24:32]], axis=0)
     dec_out[...] = (dsum + dec_in[...].astype(F32)).astype(BF16)
 
@@ -554,7 +551,6 @@
     ag1.drain()
     sc0.drain()
     sc1.drain()
-    scd.drain()
     for c in kv_join + [q_swap, s_swap, e_swap, o_swap]:
         c.wait_send()
 
@@ -565,7 +561,7 @@
 
 
 def scatter_bufs(rows):
-    h, w = (rows, FS // 2) if rows == DEC else (rows // 2, FS)
+    h, w = rows // 2, FS
     return (
         pltpu.VMEM((4, rows, FS), BF16),
         pltpu.VMEM((4, h, w), BF16),
@@ -620,9 +616,8 @@
             pltpu.VMEM((C1, HD), BF16),
             pltpu.VMEM((512, 2 * HD), BF16),
             pltpu.VMEM((DEC, 2 * HD), BF16),
-            pltpu.VMEM((256, FS), BF16),
-            pltpu.VMEM((256, FS), BF16),
-            pltpu.VMEM((DEC, FS), BF16),
+            pltpu.VMEM((T0, FS), BF16),
+            pltpu.VMEM((T1 + DEC, FS), BF16),
             pltpu.VMEM((16, 2, 64, CACHE), BF16),
             pltpu.VMEM((256, CACHE), F32),
             pltpu.VMEM((HD, CACHE), F32),
@@ -639,9 +634,8 @@
             pltpu.VMEM((DEC, FS), BF16),
             pltpu.VMEM((16, 1024), F32),
             pltpu.VMEM((8, 512), jnp.int32),
-            scatter_bufs(256),
-            scatter_bufs(256),
-            scatter_bufs(DEC),
+            scatter_bufs(T0),
+            scatter_bufs(T1 + DEC),
             pltpu.SemaphoreType.DMA((4,)),
             pltpu.SemaphoreType.DMA((2, 20)),
             pltpu.SemaphoreType.DMA((2, 20)),

time: 125 us -> 124 us (level)
  no operation moved by 1% of the time
where the time goes in v1:
time: 124 us
  Pallas kernels  119 us (96%)
  local copies, waits for them, and re-layouts  3.24 us (3%)
  between operations  1.29 us (1%)
    pallas_call x1, Pallas kernels, body(): pl.pallas_call(kernel, out_shape=(jax.ShapeDtypeStruct((512, FS), BF16),...  119 us
    unnamed x2, local copies, waits for them, and re-layouts  3.24 us

profile of v1, /device:TPU:1, one launch (start us, length us, event | category | flops | bytes accessed | tf_op | source)
XLA Modules:
  0.0 123.6 jit_solution(9565149703177247813)
XLA Ops:
  1.3 119.1 %shard_map.149 = (bf16[512,512]{1,0:T(8,128)(2,1)}, bf16[32,512]{1,0:T(8,128)(2,1)}) custom-call(bf16[512,512]{1,0:T(8,128)(2,1)} %pre_in.1, bf16[32,512]{1,0:T(8,128)(2,1)} %bitcast.10, bf16[8192]{0:T(1024)(128)(2,1)} %gain.1, bf16[512]{0:T(512)(128)(2,1)} %qbias.1, bf16[2,64]{1,0:T(2,128)(2,1)} %kvbias.1, f32[1,128]{1,0:T(1,128)} %constant.2.clone.freq, ...), custom_call_target="tpu_custom_call" | custom-call | tf_op jit(solution)/shard_map/pallas_call | solution.py:590
  120.4 1.9 %copy.19 = bf16[512,512]{1,0:T(8,128)(2,1)} copy(bf16[512,512]{1,0:T(8,128)(2,1)} %get-tuple-element.8) | data formatting | bytes 1048576
  122.3 1.4 %copy.20 = bf16[2,16,512]{2,1,0:T(8,128)(2,1)} copy(bf16[2,16,512]{2,1,0:T(8,128)(2,1)} %bitcast.11) | data formatting | bytes 65536

commit v2 on v1

--- a/solution.py
+++ b/solution.py
@@ -518,21 +518,22 @@
     q_swap.start()
     advance(1, 9, 10, 11)
     pass_keys(0, kvs0, kvr0, 0, C0)
+    cache_scores()
     for h in range(4):
         attend(q0, DEC, T0, att0, h, T0)
     loads[2].wait()
     sc0.first_hop()
     advance(1, 12, 13)
-    cache_scores()
-    advance(1, 14, 15)
+    cache_weights()
+    advance(1, 14)
+    cache_values()
+    advance(1, 15)
     finish(acc1, ss1, kvs1, q1, C0, C1)
     kv_join[1].start()
-    cache_weights()
     finish_q(acc1, ss1, q1, C0, C1)
     sc0.second_hop()
     pass_keys(1, kvs1, kvr1, C0, C1)
     send_pages()
-    cache_values()
     for h in range(4):
         attend(q1, 0, T1, att1, h, 512)
     sc0.third_hop()

time: 124 us -> 127 us (1.024)
  Pallas kernels: 119 us -> 122 us
    pallas_call x1, Pallas kernels: 119 us -> 122 us  [body(): pl.pallas_call(kernel, out_shape=(jax.ShapeDtypeStruct((512, FS), BF16),...]
where the time goes in v2:
time: 127 us
  Pallas kernels  122 us (96%)
  local copies, waits for them, and re-layouts  3.24 us (3%)
  between operations  1.29 us (1%)
    pallas_call x1, Pallas kernels, body(): pl.pallas_call(kernel, out_shape=(jax.ShapeDtypeStruct((512, FS), BF16),...  122 us
    unnamed x2, local copies, waits for them, and re-layouts  3.24 us

profile of v2, /device:TPU:1, one launch (start us, length us, event | category | flops | bytes accessed | tf_op | source)
XLA Modules:
  0.0 126.5 jit_solution(13712231707241309981)
XLA Ops:
  1.3 122.0 %shard_map.149 = (bf16[512,512]{1,0:T(8,128)(2,1)}, bf16[32,512]{1,0:T(8,128)(2,1)}) custom-call(bf16[512,512]{1,0:T(8,128)(2,1)} %pre_in.1, bf16[32,512]{1,0:T(8,128)(2,1)} %bitcast.10, bf16[8192]{0:T(1024)(128)(2,1)} %gain.1, bf16[512]{0:T(512)(128)(2,1)} %qbias.1, bf16[2,64]{1,0:T(2,128)(2,1)} %kvbias.1, f32[1,128]{1,0:T(1,128)} %constant.2.clone.freq, ...), custom_call_target="tpu_custom_call" | custom-call | tf_op jit(solution)/shard_map/pallas_call | solution.py:591
  123.3 1.9 %copy.19 = bf16[512,512]{1,0:T(8,128)(2,1)} copy(bf16[512,512]{1,0:T(8,128)(2,1)} %get-tuple-element.8) | data formatting | bytes 1048576
  125.2 1.4 %copy.20 = bf16[2,16,512]{2,1,0:T(8,128)(2,1)} copy(bf16[2,16,512]{2,1,0:T(8,128)(2,1)} %bitcast.11) | data formatting | bytes 65536

commit v3 on v1

--- a/solution.py
+++ b/solution.py
@@ -168,30 +168,6 @@
         params[i:i + 1] = gain[i * FS:(i + 1) * FS].astype(F32).reshape(1, FS)
     params[16:17] = qbias[...].astype(F32).reshape(1, FS)
     params[17:18, 0:HD] = jnp.concatenate([kvbias[0:1].astype(F32), kvbias[1:2].astype(F32)], axis=1)
-    acc0[...] = jnp.zeros_like(acc0)
-    acc1[...] = jnp.zeros_like(acc1)
-    ss0[...] = jnp.zeros_like(ss0)
-    ss1[...] = jnp.zeros_like(ss1)
-    loads[0].wait()
-    loads[1].wait()
-
-    gathers = ((ag0, x0, acc0, ss0), (ag1, x1, acc1, ss1))
-
-    def advance(c, *steps):
-        ag, x, acc, ss = gathers[c]
-        for place in [ag.step(i) for i in steps]:
-            accumulate(x, acc, ss, place)
-
-    advance(0, 0, 1, 2, 3, 4)
-    advance(0, 5)
-
-    advance(1, 0, 1, 2, 3, 4)
-    advance(0, 6, 7, 8)
-    advance(1, 5)
-    advance(0, 9, 10, 11)
-    advance(1, 6, 7, 8)
-    advance(0, 12, 13)
-
     lane = lax.broadcasted_iota(jnp.int32, (C0, HD), 1)
     row = lax.broadcasted_iota(jnp.int32, (C0, HD), 0)
     places = row - DEC + offset[0]
@@ -208,33 +184,29 @@
     cos_t[C0:C0 + C1] = jnp.cos(angle)
     sin_t[C0:C0 + C1] = jnp.sin(angle) * sign[0:1]
 
-    token = lax.broadcasted_iota(jnp.int32, (8, 512), 1)
-
-    def rank_block(b, carry):
-        slots, counts = carry
-        d = routing[b]
-        rank = jnp.int32(0)
-        for k in range(8):
-            rank = rank + jnp.where(d == k, counts[k], 0)
-        slots = jnp.where(token // 16 == b, d * 128 + rank * 16 + token % 16, slots)
-        return slots, tuple(counts[k] + jnp.where(d == k, 1, 0) for k in range(8))
-
-    slots, counts = lax.fori_loop(
-        0, 32, rank_block, (jnp.zeros((8, 512), jnp.int32), (jnp.int32(0),) * 8)
-    )
-    tok_slot[...] = slots
-    for k in range(8):
-        cnt_s[k] = jnp.full((8, 128), 1.0, F32) * counts[k].astype(F32)
-
-    page = lax.broadcasted_iota(jnp.int32, (16, 1024), 1) // 16
-    prow = lax.broadcasted_iota(jnp.int32, (16, 1024), 0)
-
-    def count_pages(i, times):
-        r, j = i // 8, i % 8
-        return times + jnp.where((prow == r) & (page == table[j, r]), 1.0, 0.0)
-
-    mult[...] = lax.fori_loop(0, 128, count_pages, jnp.zeros((16, 1024), F32))
-
+    acc0[...] = jnp.zeros_like(acc0)
+    acc1[...] = jnp.zeros_like(acc1)
+    ss0[...] = jnp.zeros_like(ss0)
+    ss1[...] = jnp.zeros_like(ss1)
+    loads[0].wait()
+    loads[1].wait()
+
+    gathers = ((ag0, x0, acc0, ss0), (ag1, x1, acc1, ss1))
+
+    def advance(c, *steps):
+        ag, x, acc, ss = gathers[c]
+        for place in [ag.step(i) for i in steps]:
+            accumulate(x, acc, ss, place)
+
+    advance(0, 0, 1, 2, 3, 4)
+    advance(0, 5)
+
+    advance(1, 0, 1, 2, 3, 4)
+    advance(0, 6, 7, 8)
+    advance(1, 5)
+    advance(0, 9, 10, 11)
+    advance(1, 6, 7, 8)
+    advance(0, 12, 13)
     advance(0, 14, 15)
 
     def finish(acc, ss, kvs, q, table_at, rows):
@@ -516,13 +488,42 @@
     kv_join[0].start()
     finish_q(acc0, ss0, q0, 0, C0)
     q_swap.start()
-    advance(1, 9, 10, 11)
+    advance(1, 9)
     pass_keys(0, kvs0, kvr0, 0, C0)
     for h in range(4):
         attend(q0, DEC, T0, att0, h, T0)
     loads[2].wait()
     sc0.first_hop()
+    advance(1, 10, 11)
     advance(1, 12, 13)
+
+    token = lax.broadcasted_iota(jnp.int32, (8, 512), 1)
+
+    def rank_block(b, carry):
+        slots, counts = carry
+        d = routing[b]
+        rank = jnp.int32(0)
+        for k in range(8):
+            rank = rank + jnp.where(d == k, counts[k], 0)
+        slots = jnp.where(token // 16 == b, d * 128 + rank * 16 + token % 16, slots)
+        return slots, tuple(counts[k] + jnp.where(d == k, 1, 0) for k in range(8))
+
+    slots, counts = lax.fori_loop(
+        0, 32, rank_block, (jnp.zeros((8, 512), jnp.int32), (jnp.int32(0),) * 8)
+    )
+    tok_slot[...] = slots
+    for k in range(8):
+        cnt_s[k] = jnp.full((8, 128), 1.0, F32) * counts[k].astype(F32)
+
+    page = lax.broadcasted_iota(jnp.int32, (16, 1024), 1) // 16
+    prow = lax.broadcasted_iota(jnp.int32, (16, 1024), 0)
+
+    def count_pages(i, times):
+        r, j = i // 8, i % 8
+        return times + jnp.where((prow == r) & (page == table[j, r]), 1.0, 0.0)
+
+    mult[...] = lax.fori_loop(0, 128, count_pages, jnp.zeros((16, 1024), F32))
+
     cache_scores()
     advance(1, 14, 15)
     finish(acc1, ss1, kvs1, q1, C0, C1)

time: 124 us -> 126 us (1.016)
  Pallas kernels: 119 us -> 121 us
    pallas_call x1, Pallas kernels: 119 us -> 121 us  [body(): pl.pallas_call(kernel, out_shape=(jax.ShapeDtypeStruct((512, FS), BF16),...]
where the time goes in v3:
time: 126 us; the launch traced here: 125 us
  Pallas kernels  121 us (96%)
  local copies, waits for them, and re-layouts  3.24 us (3%)
  between operations  1.29 us (1%)
    pallas_call x1, Pallas kernels, body(): pl.pallas_call(kernel, out_shape=(jax.ShapeDtypeStruct((512, FS), BF16),...  121 us
    unnamed x2, local copies, waits for them, and re-layouts  3.24 us

profile of v3, /device:TPU:1, one launch (start us, length us, event | category | flops | bytes accessed | tf_op | source)
XLA Modules:
  0.0 125.3 jit_solution(15574381956376684316)
XLA Ops:
  1.3 120.8 %shard_map.149 = (bf16[512,512]{1,0:T(8,128)(2,1)}, bf16[32,512]{1,0:T(8,128)(2,1)}) custom-call(bf16[512,512]{1,0:T(8,128)(2,1)} %pre_in.1, bf16[32,512]{1,0:T(8,128)(2,1)} %bitcast.10, bf16[8192]{0:T(1024)(128)(2,1)} %gain.1, bf16[512]{0:T(512)(128)(2,1)} %qbias.1, bf16[2,64]{1,0:T(2,128)(2,1)} %kvbias.1, f32[1,128]{1,0:T(1,128)} %constant.2.clone.freq, ...), custom_call_target="tpu_custom_call" | custom-call | tf_op jit(solution)/shard_map/pallas_call | solution.py:591
  122.1 1.9 %copy.19 = bf16[512,512]{1,0:T(8,128)(2,1)} copy(bf16[512,512]{1,0:T(8,128)(2,1)} %get-tuple-element.8) | data formatting | bytes 1048576
  123.9 1.4 %copy.20 = bf16[2,16,512]{2,1,0:T(8,128)(2,1)} copy(bf16[2,16,512]{2,1,0:T(8,128)(2,1)} %bitcast.11) | data formatting | bytes 65536
